TPU v7x, 32 devices: a whole 2x2x4 slice. The times are simulated.
32 devices in a mesh: fsdp: 8 (over y, x, core), tp: 4 (over z).
Axes of the slice: x: 2, y: 2, z: 4, core: 2. Of those that a mesh axis runs over, the one named last changes fastest.
Arguments:
- acts: bfloat16 [16384, 5120], P('fsdp', 'tp'), may hold values from -6 to 6
- cotangent: bfloat16 [16384, 5120], P('fsdp', 'tp'), may hold values from -6 to 6
- master: float32 [5120, 5120], P('fsdp', 'tp'), may hold values from -0.078125 to 0.078125
- moment_one: bfloat16 [5120, 5120], P('fsdp', 'tp'), may hold values from -4 to 4
- moment_two: bfloat16 [5120, 5120], P('fsdp', 'tp'), may hold values from 0.25 to 2
- queries: bfloat16 [3, 256, 5120], P(None, 'fsdp', 'tp')
- fresh_kv: bfloat16 [2, 3, 256, 1024], P(None, None, 'fsdp', 'tp')
- cache: bfloat16 [2, 256, 8, 512, 128], P(None, 'fsdp', 'tp'), may hold values from -6 to 6
- lengths: int32 [256], P('fsdp'), may hold values from 1 to 512, as said below
- draft_ids: int32 [3, 256], P(None, 'fsdp'), may hold values from 0 to 151643, as said below
Outputs:
- input_grad: bfloat16 [16384, 5120], P('fsdp', 'tp')
- master_new: float32 [5120, 5120], P('fsdp', 'tp')
- moment_one_new: bfloat16 [5120, 5120], P('fsdp', 'tp')
- moment_two_new: bfloat16 [5120, 5120], P('fsdp', 'tp')
- decoded: bfloat16 [3, 256, 5120], P(None, 'fsdp', 'tp')
Inputs may be any that keep to these rules, and one draw needn't show every extreme that they name: `lengths`: the first row of each block of 32 rows has exactly 512 valid positions. `draft_ids`: 151643 is the end-of-sequence id.
All inputs are finite; a program needn't handle non-finite values.
Results may differ from a plain program's by a relative error of at most 0.0064.
Values may be sent and summed in bfloat16 or wider, within the bound.
A program may use at most 192 MiB of HBM per device.

v0:
```python
import jax
import jax.numpy as jnp
from jax import lax
from jax.sharding import PartitionSpec as P

end_token = 151643


def alive_mask(draft_ids):
    ended = (draft_ids == end_token).astype(jnp.int32)
    first = jnp.ones_like(ended[0])
    second = 1 - ended[0]
    third = second * (1 - ended[1])
    return jnp.stack([first, second, third])


def attend_local(queries, fresh_kv, cache, lengths, draft_ids):
    steps, rows, width = queries.shape
    heads_kv = cache.shape[2]
    head_size = cache.shape[4]
    groups = width // (heads_kv * head_size)
    scale = head_size ** (-0.5)
    qs = queries.reshape(steps, rows, heads_kv, groups, head_size)
    nk = fresh_kv[0].reshape(steps, rows, heads_kv, head_size)
    nv = fresh_kv[1].reshape(steps, rows, heads_kv, head_size)
    s_cache = (
        jnp.einsum("srkgd,rkpd->rkgsp", qs, cache[0], preferred_element_type=jnp.float32) * scale
    )
    s_new = jnp.einsum("srkgd,trkd->rkgst", qs, nk, preferred_element_type=jnp.float32) * scale
    pos = lax.broadcasted_iota(jnp.int32, s_cache.shape, 4)
    keep_cache = pos < lengths[:, None, None, None, None]
    alive = alive_mask(draft_ids)
    s_idx = lax.broadcasted_iota(jnp.int32, (steps, steps), 0)
    t_idx = lax.broadcasted_iota(jnp.int32, (steps, steps), 1)
    keep_new = (t_idx <= s_idx)[None, :, :] & (alive.T[:, None, :] > 0)
    keep_new = keep_new[:, None, None, :, :]
    s_cache = jnp.where(keep_cache, s_cache, -jnp.inf)
    s_new = jnp.where(keep_new, s_new, -jnp.inf)
    top = jnp.maximum(jnp.max(s_cache, axis=4), jnp.max(s_new, axis=4))
    e_cache = jnp.exp(s_cache - top[..., None])
    e_new = jnp.exp(s_new - top[..., None])
    total = jnp.sum(e_cache, axis=4) + jnp.sum(e_new, axis=4)
    p_cache = (e_cache / total[..., None]).astype(jnp.bfloat16)
    p_new = (e_new / total[..., None]).astype(jnp.bfloat16)
    out = jnp.einsum("rkgsp,rkpd->srkgd", p_cache, cache[1], preferred_element_type=jnp.float32)
    out = out + jnp.einsum("rkgst,trkd->srkgd", p_new, nv, preferred_element_type=jnp.float32)
    return out.astype(jnp.bfloat16).reshape(steps * rows, width)


def adamw(master, moment_one, moment_two, grad):
    first = 0.9 * moment_one.astype(jnp.float32) + 0.1 * grad
    second = 0.95 * moment_two.astype(jnp.float32) + 0.05 * grad * grad
    corr_one = 1.0 - 0.9**10
    corr_two = 1.0 - 0.95**10
    updated = master - 0.001 * (
        first / corr_one / (jnp.sqrt(second / corr_two) + 1e-08) + 0.1 * master
    )
    return (updated, first.astype(jnp.bfloat16), second.astype(jnp.bfloat16))


def local(
    acts, cotangent, master, moment_one, moment_two, queries, fresh_kv, cache, lengths, draft_ids
):
    steps, rows, width_in = queries.shape
    tokens_here = acts.shape[0]
    weight = master.astype(jnp.bfloat16)
    cot_full = lax.all_gather(cotangent, "tp", axis=1, tiled=True)
    part = cot_full
    input_grad = jnp.dot(
        part, lax.all_gather(weight, "fsdp", axis=0, tiled=True), preferred_element_type=jnp.float32
    ).astype(jnp.bfloat16)
    grad_scale = float(tokens_here * lax.axis_size("fsdp")) ** (-0.5)
    attended = attend_local(queries, fresh_kv, cache, lengths, draft_ids)
    part = cot_full
    grad = (
        lax.psum_scatter(
            lax.dot_general(
                part, acts, (((0,), (0,)), ((), ())), preferred_element_type=jnp.float32
            ).astype(jnp.bfloat16),
            "fsdp",
            scatter_dimension=0,
            tiled=True,
        ).astype(jnp.float32)
        * grad_scale
    )
    master_new, moment_one_new, moment_two_new = adamw(master, moment_one, moment_two, grad)
    fresh = master_new.astype(jnp.bfloat16)
    partial_value = lax.dot_general(
        attended,
        lax.all_gather(fresh, "fsdp", axis=0, tiled=True),
        (((1,), (1,)), ((), ())),
        preferred_element_type=jnp.float32,
    )
    decoded = lax.psum_scatter(partial_value, "tp", scatter_dimension=1, tiled=True).astype(
        jnp.bfloat16
    )
    decoded = decoded.reshape(steps, rows, decoded.shape[1])
    return (input_grad, master_new, moment_one_new, moment_two_new, decoded)


def solution(mesh):
    in_specs = (
        P("fsdp", "tp"),
        P("fsdp", "tp"),
        P("fsdp", "tp"),
        P("fsdp", "tp"),
        P("fsdp", "tp"),
        P(None, "fsdp", "tp"),
        P(None, None, "fsdp", "tp"),
        P(None, "fsdp", "tp", None, None),
        P("fsdp"),
        P(None, "fsdp"),
    )
    out_specs = (
        P("fsdp", "tp"),
        P("fsdp", "tp"),
        P("fsdp", "tp"),
        P("fsdp", "tp"),
        P(None, "fsdp", "tp"),
    )
    return jax.shard_map(local, mesh=mesh, in_specs=in_specs, out_specs=out_specs, check_vma=False)
```

profile of v0, /device:TPU:3, one launch (start us, length us, event | category | flops | bytes accessed | tf_op | source)
XLA Modules:
  0.0 705.9 jit_solution(15340200015257784221)
XLA Ops:
  7.2 0.0 all-gather.4.cloned.1.call-start
  7.2 0.7 all-gather.4.cloned.1.call-update
  7.9 0.0 reduce-scatter.3.cloned.1.call-start
  7.9 359.7 %all-gather.4.cloned.1.call-done = bf16[2048,5120]{1,0:T(8,128)(2,1)} async-done(((bf16[2048,1280]{1,0:T(8,128)(2,1)}), bf16[2048,5120]{1,0:T(8,128)(2,1)}) %all-gather.4.cloned.1.call-update) | async-done | bytes 20971536 | tf_op jit(solution)/shard_map/all_gather | solution.py:67
  367.7 33.9 %convolution_convert_fusion = bf16[5120,1280]{1,0:T(8,128)(2,1)} fusion(bf16[2048,5120]{1,0:T(8,128)(2,1)} %all-gather.4.cloned.1.call-done, bf16[2048,1280]{1,0:T(8,128)(2,1)} %param.10), kind=kOutput, calls=%fused_computation | convolution fusion | flops 26850099200 | bytes 39321600 | tf_op jit(solution)/shard_map/dot_general | solution.py:77
  401.6 0.0 copy-start
  401.6 0.0 reduce-scatter.3.cloned.1.call-update
  401.6 0.0 all-gather.8.cloned.1.call-start
  401.7 93.7 %reduce-scatter.3.cloned.1.call-done = bf16[640,1280]{1,0:T(8,128)(2,1)} async-done(((bf16[5120,1280]{1,0:T(8,128)(2,1)}), bf16[640,1280]{1,0:T(8,128)(2,1)}) %reduce-scatter.3.cloned.1.call-update) | async-done | bytes 1638416 | tf_op jit(solution)/shard_map/reduce_scatter | solution.py:76
  495.4 0.0 copy-done
  495.4 8.0 %fusion.32 = (bf16[640,1280]{1,0:T(8,128)(2,1)}, f32[640,1280]{1,0:T(8,128)}, bf16[640,1280]{1,0:T(8,128)(2,1)}, bf16[640,1280]{1,0:T(8,128)(2,1)}, bf16[640,1280]{1,0:T(8,128)(2,1)}) fusion(f32[640,1280]{1,0:T(8,128)S(1)} %copy-done, bf16[640,1280]{1,0:T(8,128)(2,1)} %param.14, bf16[640,1280]{1,0:T(8,128)(2,1)} %reduce-scatter.3.cloned.1.call-done, ...), kind=kLoop, calls=%fused_computation.52 | loop fusion | flops 18841600 | bytes 18022400 | tf_op jit(solution)/shard_map/convert_element_type | solution.py:87
  503.4 0.0 copy-start.3
  503.4 0.0 copy-start.2
  503.4 0.0 copy-start.1
  503.4 0.0 copy-start.4
  503.4 0.0 all-gather.8.cloned.1.call-update
  503.4 0.0 all-gather.6.cloned.1.call-start
  503.5 0.5 all-gather.6.cloned.1.call-update
  504.0 0.2 reduce-scatter.5.cloned.1.call-start
  504.2 0.0 copy-done.3
  504.3 0.1 copy.19
  504.4 0.0 copy-done.2
  504.5 0.0 copy-done.1
  504.5 0.3 reshape.40
  504.8 1.4 fusion.34
  506.2 0.0 copy-done.4
  506.2 5.8 fusion.12
  512.0 0.4 fusion.24
  512.4 1.4 fusion.9
  513.8 5.1 fusion
  518.9 0.5 fusion.20
  519.3 0.1 copy.23
  519.4 0.3 reshape.41
  519.7 58.8 %all-gather.8.cloned.1.call-done = bf16[5120,1280]{1,0:T(8,128)(2,1)} async-done(((bf16[640,1280]{1,0:T(8,128)(2,1)}), bf16[5120,1280]{1,0:T(8,128)(2,1)}) %all-gather.8.cloned.1.call-update) | async-done | bytes 13107216 | tf_op jit(solution)/shard_map/all_gather | solution.py:90
  578.5 10.0 %fusion.35 = f32[96,5120]{1,0:T(8,128)} fusion(bf16[96,1280]{1,0:T(8,128)(2,1)S(1)} %reshape.41, bf16[5120,1280]{1,0:T(8,128)(2,1)} %all-gather.8.cloned.1.call-done), kind=kOutput, calls=%fused_computation.55 | convolution fusion | flops 1258291200 | bytes 15319040 | tf_op jit(solution)/shard_map/dot_general | solution.py:88
  588.5 0.0 reduce-scatter.5.cloned.1.call-update
  588.5 66.1 %all-gather.6.cloned.1.call-done = bf16[5120,1280]{1,0:T(8,128)(2,1)} async-done(((bf16[640,1280]{1,0:T(8,128)(2,1)}), bf16[5120,1280]{1,0:T(8,128)(2,1)}) %all-gather.6.cloned.1.call-update) | async-done | bytes 13107216 | tf_op jit(solution)/shard_map/all_gather | solution.py:70
  654.6 35.1 %convolution_convert_fusion.1 = bf16[2048,1280]{1,0:T(8,128)(2,1)} fusion(bf16[2048,5120]{1,0:T(8,128)(2,1)} %all-gather.4.cloned.1.call-done, bf16[5120,1280]{1,0:T(8,128)(2,1)} %all-gather.6.cloned.1.call-done), kind=kOutput, calls=%fused_computation.7 | convolution fusion | flops 26846167040 | bytes 39321600 | tf_op jit(solution)/shard_map/dot_general | solution.py:69
  689.7 8.0 %reduce-scatter.5.cloned.1.call-done = f32[96,1280]{1,0:T(8,128)} async-done(((f32[96,5120]{1,0:T(8,128)}), f32[96,1280]{1,0:T(8,128)}) %reduce-scatter.5.cloned.1.call-update) | async-done | bytes 491536 | tf_op jit(solution)/shard_map/reduce_scatter | solution.py:94
  697.7 1.7 convert_element_type.59
  (11 shorter events, 0.2 us)
Async XLA Ops:
  7.2 360.5 %all-gather.4.cloned.1.call-start = ((), (), s32[]{:S(2)}) async-start(), calls=%async_computation.2 | async-start | bytes 26214400 | tf_op jit(solution)/shard_map/all_gather | solution.py:67
  7.9 487.5 %reduce-scatter.3.cloned.1.call-start = ((), (), s32[]{:S(2)}) async-start(), calls=%async_computation.4 | async-start | bytes 14745600 | tf_op jit(solution)/shard_map/reduce_scatter | solution.py:76
  401.6 93.7 %copy-start = (f32[640,1280]{1,0:T(8,128)S(1)}, f32[640,1280]{1,0:T(8,128)}, u32[]{:S(2)}) copy-start(f32[640,1280]{1,0:T(8,128)} %param.12) | copy-start | bytes 9830404
  401.6 176.8 %all-gather.8.cloned.1.call-start = ((), (), s32[]{:S(2)}) async-start(), calls=%async_computation.5 | async-start | bytes 14745600 | tf_op jit(solution)/shard_map/all_gather | solution.py:90
  503.4 0.9 copy-start.3
  503.4 1.0 copy-start.2
  503.4 1.1 copy-start.1
  503.4 2.8 copy-start.4
  503.4 151.2 %all-gather.6.cloned.1.call-start = ((), (), s32[]{:S(2)}) async-start(), calls=%async_computation.3 | async-start | bytes 14745600 | tf_op jit(solution)/shard_map/all_gather | solution.py:70
  504.0 193.7 %reduce-scatter.5.cloned.1.call-start = ((), (), s32[]{:S(2)}) async-start(), calls=%async_computation.6 | async-start | bytes 2457600 | tf_op jit(solution)/shard_map/reduce_scatter | solution.py:94
Sparse Core Ops, SparseCore 0:
  9.6 358.0 all-gather.3
  401.8 93.5 reduce-scatter.2
  503.5 74.8 all-gather.7
  580.2 74.3 all-gather.5
  656.8 40.8 reduce-scatter.4
where the time goes:
time: 708 us; the launch traced here: 706 us
  waiting for transfers between devices  587 us (83%)
  matrix products  91.7 us (13%)
  between operations  13.9 us (2%)
  other arithmetic  11.6 us (2%)
    all_gather x1, waiting for transfers between devices, local(): cot_full = lax.all_gather(cotangent, 'tp', axis=1, tiled=True)  360 us
    reduce_scatter x1, waiting for transfers between devices, local(): lax.psum_scatter(lax.dot_general(part, acts, (((0,), (0,)), ((), ())), pr...  93.7 us
    all_gather x1, waiting for transfers between devices, local(): lax.all_gather(weight, 'fsdp', axis=0, tiled=True)  66.1 us
    all_gather x1, waiting for transfers between devices, local(): lax.all_gather(fresh, 'fsdp', axis=0, tiled=True)  58.8 us
    dot_general x1, matrix products, local(): jnp.dot(part, lax.all_gather(weight, 'fsdp', axis=0, tiled=True), preferr...  35.1 us
    dot_general x1, matrix products, local(): lax.dot_general(part, acts, (((0,), (0,)), ((), ())), preferred_element_t...  33.9 us
  transfers between devices with their start and end apart: 5, of which 5 were waited for; matrix products, arithmetic and copies ran while one was open for 9% of the time, Pallas kernels for 0%

commit v1 on v0

--- a/solution.py
+++ b/solution.py
@@ -58,43 +58,107 @@
     return (updated, first.astype(jnp.bfloat16), second.astype(jnp.bfloat16))
 
 
+def line_gather(block, ends):
+    count = lax.axis_size("tp")
+    me = lax.axis_index("tp")
+    low, high = (0, count - 1) if ends else (1, count - 2)
+    from_low, from_high = [], []
+    up = down = block
+    for s in range(count - 1):
+        up = lax.ppermute(up, "tp", [(p, p + 1) for p in range(s, high)])
+        down = lax.ppermute(down, "tp", [(p, p - 1) for p in range(low + 1, count - s)])
+        from_low.append(up)
+        from_high.append(down)
+    blocks = [block]
+    for k in range(1, count):
+        blocks.append(jnp.where(me + k < count, from_high[k - 1], from_low[count - 1 - k]))
+    return jnp.concatenate(blocks, axis=1)
+
+
+def rotate(array, by):
+    twice = jnp.concatenate([array, array])
+    return lax.dynamic_slice_in_dim(twice, by, array.shape[0], 0)
+
+
+def decode(attended_all, fresh, steps, rows):
+    fsdp, tp = lax.axis_size("fsdp"), lax.axis_size("tp")
+    per = fsdp // tp
+    partial_value = lax.dot_general(
+        attended_all, fresh, (((1,), (1,)), ((), ())), preferred_element_type=jnp.float32
+    ).astype(jnp.bfloat16)
+    mine = lax.psum_scatter(partial_value, "tp", scatter_dimension=0, tiled=True)
+    mine = mine.reshape(per, steps * rows, fresh.shape[0])
+    place = lax.axis_index("fsdp") % per
+    got = []
+    for s in range(per):
+        perm = []
+        for a in range(tp):
+            for b in range(per):
+                for p in range(tp):
+                    target = p * per + (b + s) % per
+                    perm.append(((a * per + b) * tp + p, target * tp + a))
+        sent = lax.dynamic_index_in_dim(mine, (place + s) % per, 0, keepdims=False)
+        got.append(lax.ppermute(sent, ("fsdp", "tp"), perm))
+    got = jnp.stack(got)
+    order = (place - jnp.arange(per)) % per
+    columns = [lax.dynamic_index_in_dim(got, order[b], 0, keepdims=False) for b in range(per)]
+    return jnp.concatenate(columns, axis=1).reshape(steps, rows, per * fresh.shape[0])
+
+
 def local(
     acts, cotangent, master, moment_one, moment_two, queries, fresh_kv, cache, lengths, draft_ids
 ):
     steps, rows, width_in = queries.shape
     tokens_here = acts.shape[0]
-    weight = master.astype(jnp.bfloat16)
-    cot_full = lax.all_gather(cotangent, "tp", axis=1, tiled=True)
-    part = cot_full
-    input_grad = jnp.dot(
-        part, lax.all_gather(weight, "fsdp", axis=0, tiled=True), preferred_element_type=jnp.float32
-    ).astype(jnp.bfloat16)
-    grad_scale = float(tokens_here * lax.axis_size("fsdp")) ** (-0.5)
+    fsdp, tp = lax.axis_size("fsdp"), lax.axis_size("tp")
+    me = lax.axis_index("tp")
+    rows_own = master.shape[0]
+    own = cotangent.shape[1] // rows_own
+    unit = rows_own // 5
+    groups = [(0, 3 * unit), (3 * unit, 5 * unit)]
+    grad_scale = float(tokens_here * fsdp) ** (-0.5)
+
+    pieces = cotangent.reshape(tokens_here, own, rows_own)
+    weight = lax.all_gather(master.astype(jnp.bfloat16), "fsdp", axis=0)
     attended = attend_local(queries, fresh_kv, cache, lengths, draft_ids)
-    part = cot_full
-    grad = (
-        lax.psum_scatter(
-            lax.dot_general(
-                part, acts, (((0,), (0,)), ((), ())), preferred_element_type=jnp.float32
-            ).astype(jnp.bfloat16),
-            "fsdp",
-            scatter_dimension=0,
-            tiled=True,
-        ).astype(jnp.float32)
-        * grad_scale
+    attended_all = lax.all_gather(attended, "fsdp", axis=0, tiled=True)
+    pieces = [
+        pieces[:, :, a:b].reshape(tokens_here, own * (b - a)) for a, b in groups
+    ]
+    pieces[1], weight, attended_all = lax.optimization_barrier((pieces[1], weight, attended_all))
+    gathered = [line_gather(piece, True) for piece in pieces]
+    weight = weight.reshape(tp, own, rows_own, width_in)
+
+    total = None
+    news = []
+    for (a, b), cot in zip(groups, gathered):
+        size = b - a
+        if total is not None:
+            cot, total = lax.optimization_barrier((cot, total))
+        grad = lax.dot_general(
+            cot, acts, (((0,), (0,)), ((), ())), preferred_element_type=jnp.float32
+        ).astype(jnp.bfloat16)
+        grad = rotate(grad.reshape(tp, own * size, width_in), (tp - me) % tp)
+        grad = lax.psum_scatter(
+            grad.reshape(fsdp * size, width_in), "fsdp", scatter_dimension=0, tiled=True
+        )
+        news.append(
+            adamw(
+                master[a:b], moment_one[a:b], moment_two[a:b], grad.astype(jnp.float32) * grad_scale
+            )
+        )
+        w = rotate(weight[:, :, a:b].reshape(tp, own * size, width_in), me)
+        term = jnp.dot(
+            cot, w.reshape(tp * own * size, width_in), preferred_element_type=jnp.float32
+        )
+        total = term if total is None else total + term
+    input_grad = total.astype(jnp.bfloat16)
+    master_new, moment_one_new, moment_two_new = (
+        jnp.concatenate([new[i] for new in news]) for i in range(3)
     )
-    master_new, moment_one_new, moment_two_new = adamw(master, moment_one, moment_two, grad)
-    fresh = master_new.astype(jnp.bfloat16)
-    partial_value = lax.dot_general(
-        attended,
-        lax.all_gather(fresh, "fsdp", axis=0, tiled=True),
-        (((1,), (1,)), ((), ())),
-        preferred_element_type=jnp.float32,
-    )
-    decoded = lax.psum_scatter(partial_value, "tp", scatter_dimension=1, tiled=True).astype(
-        jnp.bfloat16
-    )
-    decoded = decoded.reshape(steps, rows, decoded.shape[1])
+    fresh = jnp.concatenate([new[0].astype(jnp.bfloat16) for new in news])
+    fresh, input_grad = lax.optimization_barrier((fresh, input_grad))
+    decoded = decode(attended_all, fresh, steps, rows)
     return (input_grad, master_new, moment_one_new, moment_two_new, decoded)
 
 

time: 708 us -> 551 us (0.78)
  waiting for transfers between devices: 587 us -> 293 us
  other arithmetic: 11.6 us -> 60.8 us
  starting transfers between devices: 0.38 us -> 37.4 us
  local copies, waits for them, and re-layouts: 0.81 us -> 36.6 us
    all_gather x3 -> x2, waiting for transfers between devices: 485 us -> 0.01 us  [the longest x1 0.01 us: local(): attended_all = lax.all_gather(attended, 'fsdp', axis=0, tiled=True)]
    ppermute x0 -> x14, waiting for transfers between devices: none -> 244 us  [the longest x6 165 us: line_gather(): lax.ppermute(down, 'tp', [(p, p - 1) for p in range(low + 1, count - s)])]
    reduce_scatter x2 -> x3, waiting for transfers between devices: 102 us -> 48.6 us  [the longest x2 28.5 us: local(): lax.psum_scatter(grad.reshape(fsdp * size, width_in), 'fsdp', scatter_dim...]
    ppermute x0 -> x14, starting transfers between devices: none -> 37.2 us  [the longest x6 18.2 us: line_gather(): lax.ppermute(down, 'tp', [(p, p - 1) for p in range(low + 1, count - s)])]
    concatenate x0 -> x9, other arithmetic: none -> 32.2 us  [the longest x4 24.4 us: rotate(): twice = jnp.concatenate([array, array])]
    select_n x0 -> x7, other arithmetic: none -> 14 us  [the longest x6 14 us: line_gather(): jnp.where(me + k < count, from_high[k - 1], from_low[count - 1 - k])]
    slice x0 -> x7, local copies, waits for them, and re-layouts: none -> 13.1 us  [the longest x2 10.6 us: local(): w = rotate(weight[:, :, a:b].reshape(tp, own * size, width_in), me)]
    reshape x0 -> x1, local copies, waits for them, and re-layouts: none -> 10.8 us  [local(): pieces = cotangent.reshape(tokens_here, own, rows_own)]
  transfers between devices with their start and end apart: 5 -> 19, of which waited for: 5 -> 12; matrix products, arithmetic and copies ran while one was open for 9% -> 29% of each run, Pallas kernels for 0% -> 0%
where the time goes in v1:
time: 551 us; the launch traced here: 542 us
  waiting for transfers between devices  293 us (53%)
  matrix products  95.9 us (17%)
  other arithmetic  60.8 us (11%)
  starting transfers between devices  37.4 us (7%)
  local copies, waits for them, and re-layouts  36.6 us (7%)
  between operations  18.2 us (3%)
    ppermute x6, waiting for transfers between devices, line_gather(): lax.ppermute(down, 'tp', [(p, p - 1) for p in range(low + 1, count - s)])  165 us
    ppermute x6, waiting for transfers between devices, line_gather(): up = lax.ppermute(up, 'tp', [(p, p + 1) for p in range(s, high)])  67.6 us
    dot_general x2, matrix products, local(): jnp.dot(cot, w.reshape(tp * own * size, width_in), preferred_element_type...  41.5 us
    dot_general x2, matrix products, local(): lax.dot_general(cot, acts, (((0,), (0,)), ((), ())), preferred_element_ty...  39.6 us
    reduce_scatter x2, waiting for transfers between devices, local(): lax.psum_scatter(grad.reshape(fsdp * size, width_in), 'fsdp', scatter_dim...  28.5 us
    concatenate x4, other arithmetic, rotate(): twice = jnp.concatenate([array, array])  24.4 us
    reduce_scatter x1, waiting for transfers between devices, decode(): lax.psum_scatter(partial_value, 'tp', scatter_dimension=0, tiled=True)  20 us
    ppermute x6, starting transfers between devices, line_gather(): lax.ppermute(down, 'tp', [(p, p - 1) for p in range(low + 1, count - s)])  18.2 us
  transfers between devices with their start and end apart: 19, of which 12 were waited for; matrix products, arithmetic and copies ran while one was open for 29% of the time, Pallas kernels for 0%

profile of v1, /device:TPU:3, one launch (start us, length us, event | category | flops | bytes accessed | tf_op | source)
XLA Modules:
  0.0 541.9 jit_solution(2441145684881906802)
XLA Ops:
  10.2 1.4 fusion.51
  11.6 5.8 %fusion.12 = (f32[32,2,5,3]{2,3,1,0:T(4,128)S(1)}, f32[32,2,512,3,5]{2,4,3,1,0:T(8,128)S(1)}) fusion(s32[32]{0:T(128)} %param.18, bf16[3,32,2,5,128]{4,3,2,1,0:T(8,128)(2,1)S(1)} %reshape.86, bf16[2,32,2,512,128]{4,3,2,1,0:T(8,128)(2,1)} %param.17), kind=kOutput, calls=%fused_computation.39 | convolution fusion | flops 127794240 | bytes 10604800 | tf_op jit(solution)/shard_map/srkgd,rkpd->rkgsp/dot_general | solution.py:27
  19.2 4.5 fusion
  25.0 2.0 reshape.87
  28.4 10.8 %reshape.81 = bf16[2048,2,640]{2,1,0:T(2,128)(2,1)} reshape(bf16[2048,1280]{1,0:T(8,128)(2,1)} %param.11) | data formatting | bytes 10485760 | tf_op jit(solution)/shard_map/reshape | solution.py:121
  39.3 1.9 slice-done
  41.8 3.7 collective-permute-start.1
  46.8 65.2 %collective-permute-done.1 = bf16[2048,768]{1,0:T(8,128)(2,1)S(1)} collective-permute-done((bf16[2048,768]{1,0:T(8,128)(2,1)S(1)}, bf16[2048,768]{1,0:T(8,128)(2,1)S(1)}, u32[]{:S(2)}, u32[]{:S(2)}) %collective-permute-start.1) | collective-permute-done | bytes 3145760 | tf_op jit(solution)/shard_map/ppermute | solution.py:68
  112.0 2.6 collective-permute-start.2
  114.6 1.5 collective-permute-done
  117.8 2.3 collective-permute-start.3
  120.1 67.9 %collective-permute-done.4 = bf16[2048,768]{1,0:T(8,128)(2,1)} collective-permute-done((bf16[2048,768]{1,0:T(8,128)(2,1)S(1)}, bf16[2048,768]{1,0:T(8,128)(2,1)}, u32[]{:S(2)}, u32[]{:S(2)}) %collective-permute-start.4) | collective-permute-done | bytes 3145760 | tf_op jit(solution)/shard_map/ppermute | solution.py:69
  188.0 1.5 collective-permute-start.5
  189.5 1.8 copy.33
  191.4 4.0 broadcast_select_fusion.1
  195.4 2.2 broadcast_select_fusion.2
  197.6 59.8 %collective-permute-done.5 = bf16[2048,768]{1,0:T(8,128)(2,1)} collective-permute-done((bf16[2048,768]{1,0:T(8,128)(2,1)}, bf16[2048,768]{1,0:T(8,128)(2,1)}, u32[]{:S(2)}, u32[]{:S(2)}) %collective-permute-start.5) | collective-permute-done | bytes 3145760 | tf_op jit(solution)/shard_map/ppermute | solution.py:69
  257.4 4.0 broadcast_select_fusion
  261.3 2.6 collective-permute-start.7
  265.2 27.6 %convolution_convert_fusion = bf16[3072,1280]{1,0:T(8,128)(2,1)} fusion(bf16[2048,1280]{1,0:T(8,128)(2,1)} %param.10, bf16[2048,768]{1,0:T(8,128)(2,1)} %broadcast_select_fusion, bf16[2048,768]{1,0:T(8,128)(2,1)} %broadcast_select_fusion.1, bf16[2048,768]{1,0:T(8,128)(2,1)} %broadcast_select_fusion.2, bf16[2048,768]{1,0:T(8,128)(2,1)} %bitcast.87), kind=kOutput, calls=%fused_computation.5 | convolution fusion | flops 16160391168 | bytes 25690112 | tf_op jit(solution)/shard_map/dot_general | solution.py:138
  292.9 9.2 %fusion.7 = bf16[4,768,1280]{2,1,0:T(8,128)(2,1)} fusion(s32[]{:T(128)S(6)} %select_n.103, bf16[4,768,1280]{2,1,0:T(8,128)(2,1)} %bitcast.82), kind=kLoop, calls=%fused_computation.19 | loop fusion | flops 3932160 | bytes 15728644 | tf_op jit(solution)/shard_map/concatenate | solution.py:79
  302.2 2.3 collective-permute-done.7
  304.5 2.0 collective-permute-start.8
  306.5 3.3 collective-permute-done.6
  309.8 11.6 %collective-permute-start.10 = (bf16[2048,512]{1,0:T(8,128)(2,1)}, bf16[2048,512]{1,0:T(8,128)(2,1)}, u32[]{:S(2)}, u32[]{:S(2)}) collective-permute-start(bf16[2048,512]{1,0:T(8,128)(2,1)} %collective-permute-done.6), channel_id=1, source_target_pairs={{1,0},{2,1},{5,4},{6,5},{9,8},{10,9},{13,12},{14,13},{17,16},{18,1... | collective-permute-start | bytes 6291464 | tf_op jit(solution)/shard_map/ppermute | solution.py:69
  321.4 7.4 %slice.74 = bf16[4,2,384,1280]{3,2,1,0:T(8,128)(2,1)} slice(bf16[4,2,640,1280]{3,2,1,0:T(8,128)(2,1)} %bitcast.76), slice={[0:4], [0:2], [0:384], [0:1280]} | slice | bytes 15728640 | tf_op jit(solution)/shard_map/slice | solution.py:150
  328.7 9.1 %fusion.6 = bf16[4,768,1280]{2,1,0:T(8,128)(2,1)} fusion(s32[]{:T(128)S(6)} %select_n.112, bf16[4,768,1280]{2,1,0:T(8,128)(2,1)} %bitcast.71), kind=kLoop, calls=%fused_computation.18 | loop fusion | flops 3932160 | bytes 15728644 | tf_op jit(solution)/shard_map/concatenate | solution.py:79
  338.6 16.2 %collective-permute-done.10 = bf16[2048,512]{1,0:T(8,128)(2,1)} collective-permute-done((bf16[2048,512]{1,0:T(8,128)(2,1)}, bf16[2048,512]{1,0:T(8,128)(2,1)}, u32[]{:S(2)}, u32[]{:S(2)}) %collective-permute-start.10) | collective-permute-done | bytes 2097184 | tf_op jit(solution)/shard_map/ppermute | solution.py:69
  356.2 23.2 %fusion.11 = f32[2048,1280]{1,0:T(8,128)} fusion(bf16[3072,1280]{1,0:T(8,128)(2,1)} %bitcast.81, bf16[2048,768]{1,0:T(8,128)(2,1)} %broadcast_select_fusion, bf16[2048,768]{1,0:T(8,128)(2,1)} %broadcast_select_fusion.1, bf16[2048,768]{1,0:T(8,128)(2,1)} %broadcast_select_fusion.2, bf16[2048,768]{1,0:T(8,128)(2,1)} %bitcast.88), kind=kOutput, calls=%fused_computation.35 | convolution fusion | flops 16156459008 | bytes 30932992 | tf_op jit(solution)/shard_map/dot_general | solution.py:151
  379.4 1.8 broadcast_select_fusion.4
  381.2 1.8 broadcast_select_fusion.5
  383.0 16.0 %collective-permute-done.11 = bf16[2048,512]{1,0:T(8,128)(2,1)S(1)} collective-permute-done((bf16[2048,512]{1,0:T(8,128)(2,1)}, bf16[2048,512]{1,0:T(8,128)(2,1)S(1)}, u32[]{:S(2)}, u32[]{:S(2)}) %collective-permute-start.11) | collective-permute-done | bytes 2097184 | tf_op jit(solution)/shard_map/ppermute | solution.py:69
  401.5 12.0 %convolution_convert_fusion.1 = bf16[2048,1280]{1,0:T(8,128)(2,1)S(1)} fusion(bf16[2048,2048]{1,0:T(8,128)(2,1)S(1)} %pad_maximum_fusion.1, bf16[2048,1280]{1,0:T(8,128)(2,1)S(1)} %bitcast.97), kind=kOutput, calls=%fused_computation.20 | convolution fusion | flops 10740039680 | bytes 18874368 | tf_op jit(solution)/shard_map/dot_general | solution.py:138
  413.5 4.2 fusion.9
  417.8 1.8 copy-done.1
  419.7 6.4 %fusion.47 = (bf16[384,1280]{1,0:T(8,128)(2,1)}, f32[384,1280]{1,0:T(8,128)}, bf16[384,1280]{1,0:T(8,128)(2,1)}, bf16[384,1280]{1,0:T(8,128)(2,1)}) fusion(bf16[640,1280]{1,0:T(8,128)(2,1)} %param.14, bf16[384,1280]{1,0:T(8,128)(2,1)} %reduce-scatter.4.cloned.1.call-done, bf16[640,1280]{1,0:T(8,128)(2,1)} %param.13, f32[640,1280]{1,0:T(8,128)S(1)} %copy-done.1), kind=kLoop, calls=%fused_computation.103 | loop fusion | flops 10813440 | bytes 9830400 | tf_op jit(solution)/shard_map/convert_element_type | solution.py:159
  426.1 3.3 slice.75
  429.4 1.9 fusion.8
  431.2 18.3 %add_convert_fusion = bf16[2048,1280]{1,0:T(8,128)(2,1)} fusion(f32[2048,1280]{1,0:T(8,128)} %fusion.11, bf16[2048,2048]{1,0:T(8,128)(2,1)} %copy-done.2, bf16[2048,1280]{1,0:T(8,128)(2,1)S(1)} %bitcast.83), kind=kOutput, calls=%fused_computation.10 | convolution fusion | flops 10742661120 | bytes 29360128 | tf_op jit(solution)/shard_map/dot_general | solution.py:151
  449.5 28.5 %reduce-scatter.6.cloned.1.call-done = bf16[256,1280]{1,0:T(8,128)(2,1)} async-done(((bf16[2048,1280]{1,0:T(8,128)(2,1)}), bf16[256,1280]{1,0:T(8,128)(2,1)}) %reduce-scatter.6.cloned.1.call-update) | async-done | bytes 655376 | tf_op jit(solution)/shard_map/reduce_scatter | solution.py:142
  478.1 4.2 fusion.48
  484.4 2.7 convolution_convert_fusion.2
  491.3 1.9 pad_maximum_fusion.2
  493.3 20.0 %reduce-scatter.8.cloned.1.call-done = bf16[192,640]{1,0:T(8,128)(2,1)} async-done(((bf16[768,640]{1,0:T(8,128)(2,1)}), bf16[192,640]{1,0:T(8,128)(2,1)}) %reduce-scatter.8.cloned.1.call-update) | async-done | bytes 245776 | tf_op jit(solution)/shard_map/reduce_scatter | solution.py:89
  514.3 5.0 collective-permute-start.12
  519.3 2.7 pad_maximum_fusion.7
  522.0 9.5 %collective-permute-done.13 = bf16[96,640]{1,0:T(8,128)(2,1)S(1)} collective-permute-done((bf16[96,640]{1,0:T(8,128)(2,1)S(1)}, bf16[96,640]{1,0:T(8,128)(2,1)S(1)}, u32[]{:S(2)}, u32[]{:S(2)}) %collective-permute-start.13) | collective-permute-done | bytes 122912 | tf_op jit(solution)/shard_map/ppermute | solution.py:101
  531.5 2.6 collective-permute-done.12
  (87 shorter events, 21.7 us)
Async XLA Ops:
  7.2 254.2 %all-gather.4.cloned.1.call-start = ((), (), s32[]{:S(2)}) async-start(), calls=%async_computation.4 | async-start | bytes 2211840 | tf_op jit(solution)/shard_map/all_gather | solution.py:124
  11.6 6.2 %copy-start.13 = (s32[32]{0:T(128)S(1)}, s32[32]{0:T(128)}, u32[]{:S(2)}) copy-start(s32[32]{0:T(128)} %param.18) | copy-start | bytes 388
  23.7 3.3 copy-start
  27.0 234.4 %all-gather.6.cloned.1.call-start = ((), (), s32[]{:S(2)}) async-start(), calls=%async_computation.7 | async-start | bytes 14745600 | tf_op jit(solution)/shard_map/all_gather | solution.py:122
  28.4 389.4 %reduce-scatter.4.cloned.1.call-start = ((), (), s32[]{:S(2)}) async-start(), calls=%async_computation.3 | async-start | bytes 8847360 | tf_op jit(solution)/shard_map/reduce_scatter | solution.py:142
  39.3 1.9 slice-start
  41.8 3.7 copy-start.8
  41.8 147.7 %slice-start.1 = ((bf16[2048,2,640]{2,1,0:T(2,128)(2,1)}), bf16[2048,2,256]{2,1,0:T(2,128)(2,1)S(1)}, s32[]{:S(2)}) async-start(bf16[2048,2,640]{2,1,0:T(2,128)(2,1)} %reshape.81), calls=%async_computation.9 | async-start | bytes 4194304 | tf_op jit(solution)/shard_map/slice | solution.py:126
  41.8 70.2 %collective-permute-start.1 = (bf16[2048,768]{1,0:T(8,128)(2,1)S(1)}, bf16[2048,768]{1,0:T(8,128)(2,1)S(1)}, u32[]{:S(2)}, u32[]{:S(2)}) collective-permute-start(bf16[2048,768]{1,0:T(8,128)(2,1)S(1)} %bitcast.85), channel_id=1, source_target_pairs={{0,1},{1,2},{2,3},{4,5},{5,6},{6,7},{8,9},{9,10},{10,11},{12,13},{... | collective-permute-start | bytes 9437192 | tf_op jit(solution)/shard_map/ppermute | solution.py:68
  45.5 70.6 %collective-permute-start = (bf16[2048,768]{1,0:T(8,128)(2,1)S(1)}, bf16[2048,768]{1,0:T(8,128)(2,1)S(1)}, u32[]{:S(2)}, u32[]{:S(2)}) collective-permute-start(bf16[2048,768]{1,0:T(8,128)(2,1)S(1)} %bitcast.86), channel_id=1, source_target_pairs={{1,0},{2,1},{3,2},{5,4},{6,5},{7,6},{9,8},{10,9},{11,10},{13,12},{... | collective-permute-start | bytes 9437192 | tf_op jit(solution)/shard_map/ppermute | solution.py:69
  112.0 4.1 copy-start.9
  112.0 5.4 collective-permute-start.2
  116.1 1.6 copy-start.11
  116.1 71.8 %collective-permute-start.4 = (bf16[2048,768]{1,0:T(8,128)(2,1)S(1)}, bf16[2048,768]{1,0:T(8,128)(2,1)}, u32[]{:S(2)}, u32[]{:S(2)}) collective-permute-start(bf16[2048,768]{1,0:T(8,128)(2,1)S(1)} %collective-permute-done), channel_id=1, source_target_pairs={{1,0},{2,1},{5,4},{6,5},{9,8},{10,9},{13,12},{14,13},{17,16},{18,1... | collective-permute-start | bytes 9437192 | tf_op jit(solution)/shard_map/ppermute | solution.py:69
  117.8 77.6 %collective-permute-start.3 = (bf16[2048,768]{1,0:T(8,128)(2,1)}, bf16[2048,768]{1,0:T(8,128)(2,1)}, u32[]{:S(2)}, u32[]{:S(2)}) collective-permute-start(bf16[2048,768]{1,0:T(8,128)(2,1)} %collective-permute-done.2), channel_id=1, source_target_pairs={{2,3},{6,7},{10,11},{14,15},{18,19},{22,23},{26,27},{30,31}} | collective-permute-start | bytes 9437192 | tf_op jit(solution)/shard_map/ppermute | solution.py:68
  188.0 69.4 %collective-permute-start.5 = (bf16[2048,768]{1,0:T(8,128)(2,1)}, bf16[2048,768]{1,0:T(8,128)(2,1)}, u32[]{:S(2)}, u32[]{:S(2)}) collective-permute-start(bf16[2048,768]{1,0:T(8,128)(2,1)} %collective-permute-done.4), channel_id=1, source_target_pairs={{1,0},{5,4},{9,8},{13,12},{17,16},{21,20},{25,24},{29,28}} | collective-permute-start | bytes 9437192 | tf_op jit(solution)/shard_map/ppermute | solution.py:69
  191.4 4.0 copy-start.12
  195.4 62.0 %copy-start.10 = (bf16[2048,768]{1,0:T(8,128)(2,1)S(1)}, bf16[2048,768]{1,0:T(8,128)(2,1)}, u32[]{:S(2)}) copy-start(bf16[2048,768]{1,0:T(8,128)(2,1)} %copy-done.9) | copy-start | bytes 9437188
  197.6 63.8 %copy-start.3 = (bf16[256,8,2,256]{3,1,2,0:T(8,128)(2,1)S(1)}, bf16[256,8,2,256]{3,1,2,0:T(8,128)(2,1)}, u32[]{:S(2)}) copy-start(bf16[256,8,2,256]{3,1,2,0:T(8,128)(2,1)} %copy.33) | copy-start | bytes 6291460
  261.3 43.2 %collective-permute-start.7 = (bf16[2048,512]{1,0:T(8,128)(2,1)S(1)}, bf16[2048,512]{1,0:T(8,128)(2,1)}, u32[]{:S(2)}, u32[]{:S(2)}) collective-permute-start(bf16[2048,512]{1,0:T(8,128)(2,1)S(1)} %bitcast.78), channel_id=1, source_target_pairs={{0,1},{1,2},{2,3},{4,5},{5,6},{6,7},{8,9},{9,10},{10,11},{12,13},{... | collective-permute-start | bytes 6291464 | tf_op jit(solution)/shard_map/ppermute | solution.py:68
  264.0 45.8 %collective-permute-start.6 = (bf16[2048,512]{1,0:T(8,128)(2,1)S(1)}, bf16[2048,512]{1,0:T(8,128)(2,1)}, u32[]{:S(2)}, u32[]{:S(2)}) collective-permute-start(bf16[2048,512]{1,0:T(8,128)(2,1)S(1)} %bitcast.79), channel_id=1, source_target_pairs={{1,0},{2,1},{3,2},{5,4},{6,5},{7,6},{9,8},{10,9},{11,10},{13,12},{... | collective-permute-start | bytes 6291464 | tf_op jit(solution)/shard_map/ppermute | solution.py:69
  302.1 175.9 %reduce-scatter.6.cloned.1.call-start = ((), (), s32[]{:S(2)}) async-start(), calls=%async_computation.5 | async-start | bytes 5898240 | tf_op jit(solution)/shard_map/reduce_scatter | solution.py:142
  304.5 33.3 %collective-permute-start.8 = (bf16[2048,512]{1,0:T(8,128)(2,1)}, bf16[2048,512]{1,0:T(8,128)(2,1)}, u32[]{:S(2)}, u32[]{:S(2)}) collective-permute-start(bf16[2048,512]{1,0:T(8,128)(2,1)} %collective-permute-done.7), channel_id=1, source_target_pairs={{1,2},{2,3},{5,6},{6,7},{9,10},{10,11},{13,14},{14,15},{17,18},{18... | collective-permute-start | bytes 6291464 | tf_op jit(solution)/shard_map/ppermute | solution.py:68
  309.8 45.1 %collective-permute-start.10 = (bf16[2048,512]{1,0:T(8,128)(2,1)}, bf16[2048,512]{1,0:T(8,128)(2,1)}, u32[]{:S(2)}, u32[]{:S(2)}) collective-permute-start(bf16[2048,512]{1,0:T(8,128)(2,1)} %collective-permute-done.6), channel_id=1, source_target_pairs={{1,0},{2,1},{5,4},{6,5},{9,8},{10,9},{13,12},{14,13},{17,16},{18,1... | collective-permute-start | bytes 6291464 | tf_op jit(solution)/shard_map/ppermute | solution.py:69
  337.8 43.3 %collective-permute-start.9 = (bf16[2048,512]{1,0:T(8,128)(2,1)}, bf16[2048,512]{1,0:T(8,128)(2,1)S(1)}, u32[]{:S(2)}, u32[]{:S(2)}) collective-permute-start(bf16[2048,512]{1,0:T(8,128)(2,1)} %collective-permute-done.8), channel_id=1, source_target_pairs={{2,3},{6,7},{10,11},{14,15},{18,19},{22,23},{26,27},{30,31}} | collective-permute-start | bytes 6291464 | tf_op jit(solution)/shard_map/ppermute | solution.py:68
  354.9 44.1 %collective-permute-start.11 = (bf16[2048,512]{1,0:T(8,128)(2,1)}, bf16[2048,512]{1,0:T(8,128)(2,1)S(1)}, u32[]{:S(2)}, u32[]{:S(2)}) collective-permute-start(bf16[2048,512]{1,0:T(8,128)(2,1)} %collective-permute-done.10), channel_id=1, source_target_pairs={{1,0},{5,4},{9,8},{13,12},{17,16},{21,20},{25,24},{29,28}} | collective-permute-start | bytes 6291464 | tf_op jit(solution)/shard_map/ppermute | solution.py:69
  399.0 2.2 slice-start.2
  399.2 2.3 slice-start.3
  401.5 12.0 %copy-start.2 = (bf16[2048,2048]{1,0:T(8,128)(2,1)}, bf16[2048,2048]{1,0:T(8,128)(2,1)S(1)}, u32[]{:S(2)}) copy-start(bf16[2048,2048]{1,0:T(8,128)(2,1)S(1)} %pad_maximum_fusion.1) | copy-start | bytes 25165828
  417.7 1.9 copy-start.1
  417.8 95.5 %reduce-scatter.8.cloned.1.call-start = ((), (), s32[]{:S(2)}) async-start(), calls=%async_computation.6 | async-start | bytes 1228800 | tf_op jit(solution)/shard_map/reduce_scatter | solution.py:89
  478.1 4.2 copy-start.6
  478.1 4.2 copy-start.7
  482.3 2.1 copy-start.14
  484.4 6.9 %copy-start.4 = (f32[384,1280]{1,0:T(8,128)S(1)}, f32[384,1280]{1,0:T(8,128)}, u32[]{:S(2)}) copy-start(f32[384,1280]{1,0:T(8,128)} %get-tuple-element.20) | copy-start | bytes 5898244
  484.4 6.9 %copy-start.5 = (f32[256,1280]{1,0:T(8,128)S(1)}, f32[256,1280]{1,0:T(8,128)}, u32[]{:S(2)}) copy-start(f32[256,1280]{1,0:T(8,128)} %get-tuple-element.22) | copy-start | bytes 3932164
  514.3 17.2 %collective-permute-start.13 = (bf16[96,640]{1,0:T(8,128)(2,1)S(1)}, bf16[96,640]{1,0:T(8,128)(2,1)S(1)}, u32[]{:S(2)}, u32[]{:S(2)}) collective-permute-start(bf16[96,640]{1,0:T(8,128)(2,1)S(1)} %get-tuple-element.29), channel_id=1, source_target_pairs={{0,4},{1,12},{2,20},{3,28},{4,0},{5,8},{6,16},{7,24},{8,5},{9,13},... | collective-permute-start | bytes 368648 | tf_op jit(solution)/shard_map/ppermute | solution.py:101
  514.3 19.8 %collective-permute-start.12 = (bf16[96,640]{1,0:T(8,128)(2,1)S(1)}, bf16[96,640]{1,0:T(8,128)(2,1)S(1)}, u32[]{:S(2)}, u32[]{:S(2)}) collective-permute-start(bf16[96,640]{1,0:T(8,128)(2,1)S(1)} %get-tuple-element.30), channel_id=1, source_target_pairs={{0,0},{1,8},{2,16},{3,24},{4,4},{5,12},{6,20},{7,28},{8,1},{9,9},{... | collective-permute-start | bytes 368648 | tf_op jit(solution)/shard_map/ppermute | solution.py:101
Sparse Core Ops, SparseCore 0:
  27.1 28.9 all-gather.3
  58.6 74.3 all-gather.5
  302.3 73.7 reduce-scatter.3
  417.9 60.1 reduce-scatter.5
  487.2 25.9 reduce-scatter.7

commit v2 on v1

--- a/solution.py
+++ b/solution.py
@@ -56,6 +56,28 @@
         first / corr_one / (jnp.sqrt(second / corr_two) + 1e-08) + 0.1 * master
     )
     return (updated, first.astype(jnp.bfloat16), second.astype(jnp.bfloat16))
+
+
+def reduce_rows(parts_of):
+    fsdp, size, width = parts_of.shape
+    bits = fsdp.bit_length() - 1
+    me = lax.axis_index("fsdp")
+    done = []
+    for half in range(2):
+        order = [0] + (list(range(1, bits)) if half == 0 else list(range(bits - 1, 0, -1)))
+        piece = parts_of[:, :, half * (width // 2) : (half + 1) * (width // 2)]
+        left = list(range(bits - 1, -1, -1))
+        piece = piece.reshape((2,) * bits + (size, width // 2))
+        for bit in order:
+            axis = left.index(bit)
+            left.remove(bit)
+            mine = (me >> bit) & 1
+            give = lax.dynamic_index_in_dim(piece, 1 - mine, axis, keepdims=False)
+            keep = lax.dynamic_index_in_dim(piece, mine, axis, keepdims=False)
+            take = lax.ppermute(give, "fsdp", [(f, f ^ (1 << bit)) for f in range(fsdp)])
+            piece = (keep.astype(jnp.float32) + take.astype(jnp.float32)).astype(jnp.bfloat16)
+        done.append(piece)
+    return jnp.concatenate(done, axis=1)
 
 
 def line_gather(block, ends):
@@ -115,7 +137,7 @@
     rows_own = master.shape[0]
     own = cotangent.shape[1] // rows_own
     unit = rows_own // 5
-    groups = [(0, 3 * unit), (3 * unit, 5 * unit)]
+    groups = [(0, 2 * unit), (2 * unit, 4 * unit), (4 * unit, 5 * unit)]
     grad_scale = float(tokens_here * fsdp) ** (-0.5)
 
     pieces = cotangent.reshape(tokens_here, own, rows_own)
@@ -139,9 +161,12 @@
             cot, acts, (((0,), (0,)), ((), ())), preferred_element_type=jnp.float32
         ).astype(jnp.bfloat16)
         grad = rotate(grad.reshape(tp, own * size, width_in), (tp - me) % tp)
-        grad = lax.psum_scatter(
-            grad.reshape(fsdp * size, width_in), "fsdp", scatter_dimension=0, tiled=True
-        )
+        if b < rows_own or fsdp & (fsdp - 1):
+            grad = lax.psum_scatter(
+                grad.reshape(fsdp * size, width_in), "fsdp", scatter_dimension=0, tiled=True
+            )
+        else:
+            grad = reduce_rows(grad.reshape(fsdp, size, width_in))
         news.append(
             adamw(
                 master[a:b], moment_one[a:b], moment_two[a:b], grad.astype(jnp.float32) * grad_scale

time: 551 us -> 580 us (1.053)
  waiting for transfers between devices: 293 us -> 310 us
  starting transfers between devices: 37.4 us -> 51.4 us
    reduce_scatter x2, waiting for transfers between devices: 28.5 us -> 11.7 us  [local(): lax.psum_scatter(grad.reshape(fsdp * size, width_in), 'fsdp', scatter_dim...]
    ppermute x6 -> x9, waiting for transfers between devices: 165 us -> 181 us  [line_gather(): lax.ppermute(down, 'tp', [(p, p - 1) for p in range(low + 1, count - s)])]
    ppermute x6 -> x9, waiting for transfers between devices: 67.6 us -> 78.8 us  [line_gather(): up = lax.ppermute(up, 'tp', [(p, p + 1) for p in range(s, high)])]
    ppermute x0 -> x6, starting transfers between devices: none -> 10.6 us  [reduce_rows(): take = lax.ppermute(give, 'fsdp', [(f, f ^ 1 << bit) for f in range(fsdp)])]
    ppermute x6 -> x9, starting transfers between devices: 13.9 us -> 23.2 us  [line_gather(): up = lax.ppermute(up, 'tp', [(p, p + 1) for p in range(s, high)])]
    ppermute x0 -> x6, waiting for transfers between devices: none -> 7.76 us  [reduce_rows(): take = lax.ppermute(give, 'fsdp', [(f, f ^ 1 << bit) for f in range(fsdp)])]
    ppermute x6 -> x9, starting transfers between devices: 18.2 us -> 11.7 us  [line_gather(): lax.ppermute(down, 'tp', [(p, p - 1) for p in range(low + 1, count - s)])]
    dot_general x2 -> x3, matrix products: 39.6 us -> 34.9 us  [local(): lax.dot_general(cot, acts, (((0,), (0,)), ((), ())), preferred_element_ty...]
  transfers between devices with their start and end apart: 19 -> 31, of which waited for: 12 -> 17; matrix products, arithmetic and copies ran while one was open for 29% -> 27% of each run, Pallas kernels for 0% -> 0%
where the time goes in v2:
time: 580 us; the launch traced here: 570 us
  waiting for transfers between devices  310 us (53%)
  matrix products  92.3 us (16%)
  other arithmetic  58.8 us (10%)
  starting transfers between devices  51.4 us (9%)
  local copies, waits for them, and re-layouts  38.4 us (7%)
  between operations  18.9 us (3%)
    ppermute x9, waiting for transfers between devices, line_gather(): lax.ppermute(down, 'tp', [(p, p - 1) for p in range(low + 1, count - s)])  181 us
    ppermute x9, waiting for transfers between devices, line_gather(): up = lax.ppermute(up, 'tp', [(p, p + 1) for p in range(s, high)])  78.8 us
    dot_general x3, matrix products, local(): jnp.dot(cot, w.reshape(tp * own * size, width_in), preferred_element_type...  42.6 us
    dot_general x3, matrix products, local(): lax.dot_general(cot, acts, (((0,), (0,)), ((), ())), preferred_element_ty...  34.9 us
    ppermute x9, starting transfers between devices, line_gather(): up = lax.ppermute(up, 'tp', [(p, p + 1) for p in range(s, high)])  23.2 us
    concatenate x6, other arithmetic, rotate(): twice = jnp.concatenate([array, array])  20.4 us
    reduce_scatter x1, waiting for transfers between devices, decode(): lax.psum_scatter(partial_value, 'tp', scatter_dimension=0, tiled=True)  18.4 us
    select_n x9, other arithmetic, line_gather(): jnp.where(me + k < count, from_high[k - 1], from_low[count - 1 - k])  14.5 us
  transfers between devices with their start and end apart: 31, of which 17 were waited for; matrix products, arithmetic and copies ran while one was open for 27% of the time, Pallas kernels for 0%

profile of v2, /device:TPU:3, one launch (start us, length us, event | category | flops | bytes accessed | tf_op | source)
XLA Modules:
  0.0 570.2 jit_solution(3200970640919048283)
XLA Ops:
  11.6 5.8 %fusion.13 = (f32[32,2,5,3]{2,3,1,0:T(4,128)S(1)}, f32[32,2,512,3,5]{2,4,3,1,0:T(8,128)S(1)}) fusion(s32[32]{0:T(128)} %param.18, bf16[3,32,2,5,128]{4,3,2,1,0:T(8,128)(2,1)S(1)} %reshape.119, bf16[2,32,2,512,128]{4,3,2,1,0:T(8,128)(2,1)} %param.17), kind=kOutput, calls=%fused_computation.44 | convolution fusion | flops 127794240 | bytes 10604800 | tf_op jit(solution)/shard_map/srkgd,rkpd->rkgsp/dot_general | solution.py:27
  19.2 4.5 fusion
  28.4 10.8 %reshape.114 = bf16[2048,2,640]{2,1,0:T(2,128)(2,1)} reshape(bf16[2048,1280]{1,0:T(8,128)(2,1)} %param.11) | data formatting | bytes 10485760 | tf_op jit(solution)/shard_map/reshape | solution.py:143
  39.3 4.7 fusion.64
  44.5 4.5 collective-permute-start.1
  50.5 4.1 collective-permute-start.13
  55.8 36.1 %collective-permute-done.1 = bf16[2048,512]{1,0:T(8,128)(2,1)} collective-permute-done((bf16[2048,512]{1,0:T(8,128)(2,1)S(1)}, bf16[2048,512]{1,0:T(8,128)(2,1)}, u32[]{:S(2)}, u32[]{:S(2)}) %collective-permute-start.1) | collective-permute-done | bytes 2097184 | tf_op jit(solution)/shard_map/ppermute | solution.py:90
  92.0 2.1 collective-permute-start.2
  94.1 20.4 %collective-permute-done.13 = bf16[2048,256]{1,0:T(8,128)(2,1)S(1)} collective-permute-done((bf16[2048,256]{1,0:T(8,128)(2,1)S(1)}, bf16[2048,256]{1,0:T(8,128)(2,1)S(1)}, u32[]{:S(2)}, u32[]{:S(2)}) %collective-permute-start.13) | collective-permute-done | bytes 1048608 | tf_op jit(solution)/shard_map/ppermute | solution.py:90
  116.1 3.6 collective-permute-done.12
  125.7 18.4 %collective-permute-done.16 = bf16[2048,256]{1,0:T(8,128)(2,1)} collective-permute-done((bf16[2048,256]{1,0:T(8,128)(2,1)}, bf16[2048,256]{1,0:T(8,128)(2,1)}, u32[]{:S(2)}, u32[]{:S(2)}) %collective-permute-start.16) | collective-permute-done | bytes 1048608 | tf_op jit(solution)/shard_map/ppermute | solution.py:91
  149.1 39.9 %collective-permute-done.4 = bf16[2048,512]{1,0:T(8,128)(2,1)} collective-permute-done((bf16[2048,512]{1,0:T(8,128)(2,1)}, bf16[2048,512]{1,0:T(8,128)(2,1)}, u32[]{:S(2)}, u32[]{:S(2)}) %collective-permute-start.4) | collective-permute-done | bytes 2097184 | tf_op jit(solution)/shard_map/ppermute | solution.py:91
  190.3 21.6 %collective-permute-done.17 = bf16[2048,256]{1,0:T(8,128)(2,1)S(1)} collective-permute-done((bf16[2048,256]{1,0:T(8,128)(2,1)}, bf16[2048,256]{1,0:T(8,128)(2,1)S(1)}, u32[]{:S(2)}, u32[]{:S(2)}) %collective-permute-start.17) | collective-permute-done | bytes 1048608 | tf_op jit(solution)/shard_map/ppermute | solution.py:91
  212.1 2.3 pad_maximum_fusion.2
  214.4 3.2 broadcast_select_fusion.3
  217.5 3.1 broadcast_select_fusion.5
  220.7 36.2 %collective-permute-done.5 = bf16[2048,512]{1,0:T(8,128)(2,1)S(1)} collective-permute-done((bf16[2048,512]{1,0:T(8,128)(2,1)}, bf16[2048,512]{1,0:T(8,128)(2,1)S(1)}, u32[]{:S(2)}, u32[]{:S(2)}) %collective-permute-start.5) | collective-permute-done | bytes 2097184 | tf_op jit(solution)/shard_map/ppermute | solution.py:91
  258.5 4.3 collective-permute-start.7
  262.7 17.1 %convolution_convert_fusion.1 = bf16[2048,1280]{1,0:T(8,128)(2,1)S(1)} fusion(bf16[2048,1280]{1,0:T(8,128)(2,1)} %param.10, bf16[2048,512]{1,0:T(8,128)(2,1)} %broadcast_select_fusion.1, bf16[2048,512]{1,0:T(8,128)(2,1)} %broadcast_select_fusion.3, bf16[2048,512]{1,0:T(8,128)(2,1)} %broadcast_select_fusion.5, bf16[2048,512]{1,0:T(8,128)(2,1)} %bitcast.147), kind=kOutput, calls=%fused_computation.19 | convolution fusion | flops 10773594112 | bytes 18874368 | tf_op jit(solution)/shard_map/dot_general | solution.py:160
  281.2 22.3 %collective-permute-done.7 = bf16[2048,512]{1,0:T(8,128)(2,1)} collective-permute-done((bf16[2048,512]{1,0:T(8,128)(2,1)S(1)}, bf16[2048,512]{1,0:T(8,128)(2,1)}, u32[]{:S(2)}, u32[]{:S(2)}) %collective-permute-start.7) | collective-permute-done | bytes 2097184 | tf_op jit(solution)/shard_map/ppermute | solution.py:90
  305.4 4.3 fusion.9
  310.2 9.0 %fusion.63 = (bf16[4,2,256,1280]{3,2,1,0:T(8,128)(2,1)}, bf16[4,2,256,1280]{3,2,1,0:T(8,128)(2,1)}) fusion(bf16[4,2,640,1280]{3,2,1,0:T(8,128)(2,1)} %bitcast.123), kind=kLoop, calls=%fused_computation.147 | loop fusion | bytes 20971520 | tf_op jit(solution)/shard_map/slice | solution.py:175
  319.2 4.3 fusion.8
  323.5 2.4 collective-permute-done.6
  329.2 16.1 %fusion.19 = f32[2048,1280]{1,0:T(8,128)} fusion(bf16[2048,1280]{1,0:T(8,128)(2,1)S(1)} %bitcast.137, bf16[2048,512]{1,0:T(8,128)(2,1)} %broadcast_select_fusion.1, bf16[2048,512]{1,0:T(8,128)(2,1)} %broadcast_select_fusion.3, bf16[2048,512]{1,0:T(8,128)(2,1)} %broadcast_select_fusion.5, bf16[2048,512]{1,0:T(8,128)(2,1)} %bitcast.148), kind=kOutput, calls=%fused_computation.60 | convolution fusion | flops 10770972672 | bytes 24117248 | tf_op jit(solution)/shard_map/dot_general | solution.py:176
  345.4 2.0 slice.107
  347.4 26.5 %collective-permute-done.10 = bf16[2048,512]{1,0:T(8,128)(2,1)} collective-permute-done((bf16[2048,512]{1,0:T(8,128)(2,1)}, bf16[2048,512]{1,0:T(8,128)(2,1)}, u32[]{:S(2)}, u32[]{:S(2)}) %collective-permute-start.10) | collective-permute-done | bytes 2097184 | tf_op jit(solution)/shard_map/ppermute | solution.py:91
  375.4 2.4 fusion.11
  377.8 4.2 fusion.6
  385.7 32.6 %collective-permute-done.11 = bf16[2048,512]{1,0:T(8,128)(2,1)S(1)} collective-permute-done((bf16[2048,512]{1,0:T(8,128)(2,1)}, bf16[2048,512]{1,0:T(8,128)(2,1)S(1)}, u32[]{:S(2)}, u32[]{:S(2)}) %collective-permute-start.11) | collective-permute-done | bytes 2097184 | tf_op jit(solution)/shard_map/ppermute | solution.py:91
  420.9 11.8 %convolution_convert_fusion = bf16[2048,1280]{1,0:T(8,128)(2,1)S(1)} fusion(bf16[2048,2048]{1,0:T(8,128)(2,1)S(1)} %pad_maximum_fusion.1, bf16[2048,1280]{1,0:T(8,128)(2,1)S(1)} %bitcast.157), kind=kOutput, calls=%fused_computation.18 | convolution fusion | flops 10740039680 | bytes 18874368 | tf_op jit(solution)/shard_map/dot_general | solution.py:160
  432.7 4.1 fusion.7
  437.2 18.9 %convolution_add_fusion = f32[2048,1280]{1,0:T(8,128)} fusion(f32[2048,1280]{1,0:T(8,128)} %fusion.19, bf16[2048,2048]{1,0:T(8,128)(2,1)} %copy-done.2, bf16[2048,1280]{1,0:T(8,128)(2,1)} %bitcast.136), kind=kOutput, calls=%fused_computation.9 | convolution fusion | flops 10740039680 | bytes 34603008 | tf_op jit(solution)/shard_map/dot_general | solution.py:176
  456.1 6.0 %convolution_convert_fusion.2 = bf16[1024,1280]{1,0:T(8,128)(2,1)S(1)} fusion(bf16[2048,1024]{1,0:T(8,128)(2,1)S(1)} %copy-done.6, bf16[2048,1280]{1,0:T(8,128)(2,1)S(1)} %bitcast.159), kind=kOutput, calls=%fused_computation.29 | convolution fusion | flops 5370019840 | bytes 12058624 | tf_op jit(solution)/shard_map/dot_general | solution.py:160
  463.5 6.2 %collective-permute-start.18 = (bf16[2,2,128,640]{3,2,1,0:T(8,128)(2,1)S(1)}, bf16[2,2,128,640]{3,2,1,0:T(8,128)(2,1)S(1)}, u32[]{:S(2)}, u32[]{:S(2)}) collective-permute-start(bf16[2,2,128,640]{3,2,1,0:T(8,128)(2,1)S(1)} %dynamic-slice_bitcast_fusion.1), channel_id=1, source_target_pairs={{0,4},{4,0},{8,12},{12,8},{16,20},{20,16},{24,28},{28,24},{1,5},{5... | collective-permute-start | bytes 1966088 | tf_op jit(solution)/shard_map/ppermute | solution.py:77
  469.9 7.6 %add_convert_fusion = bf16[2048,1280]{1,0:T(8,128)(2,1)} fusion(f32[2048,1280]{1,0:T(8,128)S(1)} %copy-done.16, bf16[2048,1024]{1,0:T(8,128)(2,1)S(1)} %copy-done.6, bf16[1024,1280]{1,0:T(8,128)(2,1)S(1)} %bitcast.143), kind=kOutput, calls=%fused_computation.8 | convolution fusion | flops 5373952000 | bytes 22544384 | tf_op jit(solution)/shard_map/dot_general | solution.py:176
  479.5 4.2 collective-permute-done.19
  486.6 3.6 collective-permute-done.20
  490.3 3.0 fusion.62
  493.3 11.7 %reduce-scatter.6.cloned.1.call-done = bf16[256,1280]{1,0:T(8,128)(2,1)} async-done(((bf16[2048,1280]{1,0:T(8,128)(2,1)}), bf16[256,1280]{1,0:T(8,128)(2,1)}) %reduce-scatter.6.cloned.1.call-update) | async-done | bytes 655376 | tf_op jit(solution)/shard_map/reduce_scatter | solution.py:165
  505.0 5.4 fusion.60
  512.6 2.7 convolution_convert_fusion.3
  520.0 3.1 pad_maximum_fusion.3
  523.1 18.4 %reduce-scatter.8.cloned.1.call-done = bf16[192,640]{1,0:T(8,128)(2,1)} async-done(((bf16[768,640]{1,0:T(8,128)(2,1)}), bf16[192,640]{1,0:T(8,128)(2,1)}) %reduce-scatter.8.cloned.1.call-update) | async-done | bytes 245776 | tf_op jit(solution)/shard_map/reduce_scatter | solution.py:111
  542.5 5.0 collective-permute-start.24
  547.5 2.5 pad_maximum_fusion.6
  550.0 9.7 %collective-permute-done.25 = bf16[96,640]{1,0:T(8,128)(2,1)S(1)} collective-permute-done((bf16[96,640]{1,0:T(8,128)(2,1)S(1)}, bf16[96,640]{1,0:T(8,128)(2,1)S(1)}, u32[]{:S(2)}, u32[]{:S(2)}) %collective-permute-start.25) | collective-permute-done | bytes 122912 | tf_op jit(solution)/shard_map/ppermute | solution.py:123
  559.7 2.6 collective-permute-done.24
  (146 shorter events, 55.8 us)
Async XLA Ops:
  7.2 251.3 %all-gather.4.cloned.1.call-start = ((), (), s32[]{:S(2)}) async-start(), calls=%async_computation.4 | async-start | bytes 2211840 | tf_op jit(solution)/shard_map/all_gather | solution.py:146
  27.0 231.5 %all-gather.6.cloned.1.call-start = ((), (), s32[]{:S(2)}) async-start(), calls=%async_computation.7 | async-start | bytes 14745600 | tf_op jit(solution)/shard_map/all_gather | solution.py:144
  28.4 464.9 %reduce-scatter.4.cloned.1.call-start = ((), (), s32[]{:S(2)}) async-start(), calls=%async_computation.3 | async-start | bytes 5898240 | tf_op jit(solution)/shard_map/reduce_scatter | solution.py:165
  44.0 6.4 %slice-start.2 = ((bf16[2048,2,640]{2,1,0:T(2,128)(2,1)}), bf16[2048,2,128]{2,1,0:T(2,128)(2,1)S(1)}, s32[]{:S(2)}) async-start(bf16[2048,2,640]{2,1,0:T(2,128)(2,1)} %reshape.114), calls=%async_computation.10 | async-start | bytes 2097152 | tf_op jit(solution)/shard_map/slice | solution.py:148
  44.5 75.2 %copy-start.9 = (bf16[256,8,2,256]{3,1,2,0:T(8,128)(2,1)}, bf16[256,8,2,256]{3,1,2,0:T(8,128)(2,1)S(1)}, u32[]{:S(2)}) copy-start(bf16[256,8,2,256]{3,1,2,0:T(8,128)(2,1)S(1)} %copy.34) | copy-start | bytes 6291460
  44.5 47.5 %collective-permute-start.1 = (bf16[2048,512]{1,0:T(8,128)(2,1)S(1)}, bf16[2048,512]{1,0:T(8,128)(2,1)}, u32[]{:S(2)}, u32[]{:S(2)}) collective-permute-start(bf16[2048,512]{1,0:T(8,128)(2,1)S(1)} %bitcast.145), channel_id=1, source_target_pairs={{0,1},{1,2},{2,3},{4,5},{5,6},{6,7},{8,9},{9,10},{10,11},{12,13},{... | collective-permute-start | bytes 6291464 | tf_op jit(solution)/shard_map/ppermute | solution.py:90
  49.0 71.9 %collective-permute-start = (bf16[2048,512]{1,0:T(8,128)(2,1)S(1)}, bf16[2048,512]{1,0:T(8,128)(2,1)}, u32[]{:S(2)}, u32[]{:S(2)}) collective-permute-start(bf16[2048,512]{1,0:T(8,128)(2,1)S(1)} %bitcast.146), channel_id=1, source_target_pairs={{1,0},{2,1},{3,2},{5,4},{6,5},{7,6},{9,8},{10,9},{11,10},{13,12},{... | collective-permute-start | bytes 6291464 | tf_op jit(solution)/shard_map/ppermute | solution.py:91
  50.5 64.0 %collective-permute-start.13 = (bf16[2048,256]{1,0:T(8,128)(2,1)S(1)}, bf16[2048,256]{1,0:T(8,128)(2,1)S(1)}, u32[]{:S(2)}, u32[]{:S(2)}) collective-permute-start(bf16[2048,256]{1,0:T(8,128)(2,1)S(1)} %bitcast.140), channel_id=1, source_target_pairs={{0,1},{1,2},{2,3},{4,5},{5,6},{6,7},{8,9},{9,10},{10,11},{12,13},{... | collective-permute-start | bytes 3145736 | tf_op jit(solution)/shard_map/ppermute | solution.py:90
  54.5 65.1 %collective-permute-start.12 = (bf16[2048,256]{1,0:T(8,128)(2,1)S(1)}, bf16[2048,256]{1,0:T(8,128)(2,1)}, u32[]{:S(2)}, u32[]{:S(2)}) collective-permute-start(bf16[2048,256]{1,0:T(8,128)(2,1)S(1)} %bitcast.141), channel_id=1, source_target_pairs={{1,0},{2,1},{3,2},{5,4},{6,5},{7,6},{9,8},{10,9},{11,10},{13,12},{... | collective-permute-start | bytes 3145736 | tf_op jit(solution)/shard_map/ppermute | solution.py:91
  92.0 53.4 %collective-permute-start.2 = (bf16[2048,512]{1,0:T(8,128)(2,1)}, bf16[2048,512]{1,0:T(8,128)(2,1)}, u32[]{:S(2)}, u32[]{:S(2)}) collective-permute-start(bf16[2048,512]{1,0:T(8,128)(2,1)} %collective-permute-done.1), channel_id=1, source_target_pairs={{1,2},{2,3},{5,6},{6,7},{9,10},{10,11},{13,14},{14,15},{17,18},{18... | collective-permute-start | bytes 6291464 | tf_op jit(solution)/shard_map/ppermute | solution.py:90
  114.5 6.5 %copy-start.12 = (bf16[2048,256]{1,0:T(8,128)(2,1)}, bf16[2048,256]{1,0:T(8,128)(2,1)S(1)}, u32[]{:S(2)}) copy-start(bf16[2048,256]{1,0:T(8,128)(2,1)S(1)} %collective-permute-done.13) | copy-start | bytes 3145732
  114.5 7.8 %collective-permute-start.14 = (bf16[2048,256]{1,0:T(8,128)(2,1)S(1)}, bf16[2048,256]{1,0:T(8,128)(2,1)}, u32[]{:S(2)}, u32[]{:S(2)}) collective-permute-start(bf16[2048,256]{1,0:T(8,128)(2,1)S(1)} %collective-permute-done.13), channel_id=1, source_target_pairs={{1,2},{2,3},{5,6},{6,7},{9,10},{10,11},{13,14},{14,15},{17,18},{18... | collective-permute-start | bytes 3145736 | tf_op jit(solution)/shard_map/ppermute | solution.py:90
  119.7 24.4 %collective-permute-start.16 = (bf16[2048,256]{1,0:T(8,128)(2,1)}, bf16[2048,256]{1,0:T(8,128)(2,1)}, u32[]{:S(2)}, u32[]{:S(2)}) collective-permute-start(bf16[2048,256]{1,0:T(8,128)(2,1)} %collective-permute-done.12), channel_id=1, source_target_pairs={{1,0},{2,1},{5,4},{6,5},{9,8},{10,9},{13,12},{14,13},{17,16},{18,1... | collective-permute-start | bytes 3145736 | tf_op jit(solution)/shard_map/ppermute | solution.py:91
  121.0 68.1 %collective-permute-start.4 = (bf16[2048,512]{1,0:T(8,128)(2,1)}, bf16[2048,512]{1,0:T(8,128)(2,1)}, u32[]{:S(2)}, u32[]{:S(2)}) collective-permute-start(bf16[2048,512]{1,0:T(8,128)(2,1)} %collective-permute-done), channel_id=1, source_target_pairs={{1,0},{2,1},{5,4},{6,5},{9,8},{10,9},{13,12},{14,13},{17,16},{18,1... | collective-permute-start | bytes 6291464 | tf_op jit(solution)/shard_map/ppermute | solution.py:91
  122.3 25.5 %collective-permute-start.15 = (bf16[2048,256]{1,0:T(8,128)(2,1)}, bf16[2048,256]{1,0:T(8,128)(2,1)}, u32[]{:S(2)}, u32[]{:S(2)}) collective-permute-start(bf16[2048,256]{1,0:T(8,128)(2,1)} %collective-permute-done.14), channel_id=1, source_target_pairs={{2,3},{6,7},{10,11},{14,15},{18,19},{22,23},{26,27},{30,31}} | collective-permute-start | bytes 3145736 | tf_op jit(solution)/shard_map/ppermute | solution.py:90
  125.7 86.2 %copy-start.13 = (bf16[2048,256]{1,0:T(8,128)(2,1)S(1)}, bf16[2048,256]{1,0:T(8,128)(2,1)}, u32[]{:S(2)}) copy-start(bf16[2048,256]{1,0:T(8,128)(2,1)} %copy-done.12) | copy-start | bytes 3145732
  144.1 67.9 %collective-permute-start.17 = (bf16[2048,256]{1,0:T(8,128)(2,1)}, bf16[2048,256]{1,0:T(8,128)(2,1)S(1)}, u32[]{:S(2)}, u32[]{:S(2)}) collective-permute-start(bf16[2048,256]{1,0:T(8,128)(2,1)} %collective-permute-done.16), channel_id=1, source_target_pairs={{1,0},{5,4},{9,8},{13,12},{17,16},{21,20},{25,24},{29,28}} | collective-permute-start | bytes 3145736 | tf_op jit(solution)/shard_map/ppermute | solution.py:91
  145.4 72.1 %collective-permute-start.3 = (bf16[2048,512]{1,0:T(8,128)(2,1)}, bf16[2048,512]{1,0:T(8,128)(2,1)S(1)}, u32[]{:S(2)}, u32[]{:S(2)}) collective-permute-start(bf16[2048,512]{1,0:T(8,128)(2,1)} %collective-permute-done.2), channel_id=1, source_target_pairs={{2,3},{6,7},{10,11},{14,15},{18,19},{22,23},{26,27},{30,31}} | collective-permute-start | bytes 6291464 | tf_op jit(solution)/shard_map/ppermute | solution.py:90
  189.1 67.9 %collective-permute-start.5 = (bf16[2048,512]{1,0:T(8,128)(2,1)}, bf16[2048,512]{1,0:T(8,128)(2,1)S(1)}, u32[]{:S(2)}, u32[]{:S(2)}) collective-permute-start(bf16[2048,512]{1,0:T(8,128)(2,1)} %collective-permute-done.4), channel_id=1, source_target_pairs={{1,0},{5,4},{9,8},{13,12},{17,16},{21,20},{25,24},{29,28}} | collective-permute-start | bytes 6291464 | tf_op jit(solution)/shard_map/ppermute | solution.py:91
  220.7 37.8 %copy-start.3 = (bf16[256,8,2,256]{3,1,2,0:T(8,128)(2,1)S(1)}, bf16[256,8,2,256]{3,1,2,0:T(8,128)(2,1)}, u32[]{:S(2)}) copy-start(bf16[256,8,2,256]{3,1,2,0:T(8,128)(2,1)} %copy.35) | copy-start | bytes 6291460
  258.5 45.0 %collective-permute-start.7 = (bf16[2048,512]{1,0:T(8,128)(2,1)S(1)}, bf16[2048,512]{1,0:T(8,128)(2,1)}, u32[]{:S(2)}, u32[]{:S(2)}) collective-permute-start(bf16[2048,512]{1,0:T(8,128)(2,1)S(1)} %bitcast.129), channel_id=1, source_target_pairs={{0,1},{1,2},{2,3},{4,5},{5,6},{6,7},{8,9},{9,10},{10,11},{12,13},{... | collective-permute-start | bytes 6291464 | tf_op jit(solution)/shard_map/ppermute | solution.py:90
  279.9 46.1 %collective-permute-start.6 = (bf16[2048,512]{1,0:T(8,128)(2,1)S(1)}, bf16[2048,512]{1,0:T(8,128)(2,1)}, u32[]{:S(2)}, u32[]{:S(2)}) collective-permute-start(bf16[2048,512]{1,0:T(8,128)(2,1)S(1)} %bitcast.130), channel_id=1, source_target_pairs={{1,0},{2,1},{3,2},{5,4},{6,5},{7,6},{9,8},{10,9},{11,10},{13,12},{... | collective-permute-start | bytes 6291464 | tf_op jit(solution)/shard_map/ppermute | solution.py:91
  303.5 23.8 %collective-permute-start.8 = (bf16[2048,512]{1,0:T(8,128)(2,1)}, bf16[2048,512]{1,0:T(8,128)(2,1)}, u32[]{:S(2)}, u32[]{:S(2)}) collective-permute-start(bf16[2048,512]{1,0:T(8,128)(2,1)} %collective-permute-done.7), channel_id=1, source_target_pairs={{1,2},{2,3},{5,6},{6,7},{9,10},{10,11},{13,14},{14,15},{17,18},{18... | collective-permute-start | bytes 6291464 | tf_op jit(solution)/shard_map/ppermute | solution.py:90
  309.7 195.3 %reduce-scatter.6.cloned.1.call-start = ((), (), s32[]{:S(2)}) async-start(), calls=%async_computation.5 | async-start | bytes 5898240 | tf_op jit(solution)/shard_map/reduce_scatter | solution.py:165
  326.0 47.9 %collective-permute-start.10 = (bf16[2048,512]{1,0:T(8,128)(2,1)}, bf16[2048,512]{1,0:T(8,128)(2,1)}, u32[]{:S(2)}, u32[]{:S(2)}) collective-permute-start(bf16[2048,512]{1,0:T(8,128)(2,1)} %collective-permute-done.6), channel_id=1, source_target_pairs={{1,0},{2,1},{5,4},{6,5},{9,8},{10,9},{13,12},{14,13},{17,16},{18,1... | collective-permute-start | bytes 6291464 | tf_op jit(solution)/shard_map/ppermute | solution.py:91
  327.3 56.6 %collective-permute-start.9 = (bf16[2048,512]{1,0:T(8,128)(2,1)}, bf16[2048,512]{1,0:T(8,128)(2,1)}, u32[]{:S(2)}, u32[]{:S(2)}) collective-permute-start(bf16[2048,512]{1,0:T(8,128)(2,1)} %collective-permute-done.8), channel_id=1, source_target_pairs={{2,3},{6,7},{10,11},{14,15},{18,19},{22,23},{26,27},{30,31}} | collective-permute-start | bytes 6291464 | tf_op jit(solution)/shard_map/ppermute | solution.py:90
  329.2 48.6 %slice-start = ((s8[5242880]{0:T(1024)(128)(4,1)}), s8[4194304]{0:T(1024)(128)(4,1)S(1)}, s32[]{:S(2)}) async-start(s8[5242880]{0:T(1024)(128)(4,1)} %bitcast.118), calls=%async_computation.8 | async-start | bytes 8388608
  329.2 48.6 %slice-start.1 = ((s8[5242880]{0:T(1024)(128)(4,1)}), s8[1048576]{0:T(1024)(128)(4,1)S(1)}, s32[]{:S(2)}) async-start(s8[5242880]{0:T(1024)(128)(4,1)} %bitcast.118), calls=%async_computation.9 | async-start | bytes 2097152
  373.9 44.4 %collective-permute-start.11 = (bf16[2048,512]{1,0:T(8,128)(2,1)}, bf16[2048,512]{1,0:T(8,128)(2,1)S(1)}, u32[]{:S(2)}, u32[]{:S(2)}) collective-permute-start(bf16[2048,512]{1,0:T(8,128)(2,1)} %collective-permute-done.10), channel_id=1, source_target_pairs={{1,0},{5,4},{9,8},{13,12},{17,16},{21,20},{25,24},{29,28}} | collective-permute-start | bytes 6291464 | tf_op jit(solution)/shard_map/ppermute | solution.py:91
  420.9 11.8 %copy-start.2 = (bf16[2048,2048]{1,0:T(8,128)(2,1)}, bf16[2048,2048]{1,0:T(8,128)(2,1)S(1)}, u32[]{:S(2)}) copy-start(bf16[2048,2048]{1,0:T(8,128)(2,1)S(1)} %pad_maximum_fusion.1) | copy-start | bytes 25165828
  432.7 23.3 %slice-start.5 = ((s8[5242880]{0:T(1024)(128)(4,1)}), s8[1048576]{0:T(1024)(128)(4,1)S(1)}, s32[]{:S(2)}) async-start(s8[5242880]{0:T(1024)(128)(4,1)} %bitcast.158), calls=%async_computation.13 | async-start | bytes 2097152
  436.9 104.6 %reduce-scatter.8.cloned.1.call-start = ((), (), s32[]{:S(2)}) async-start(), calls=%async_computation.6 | async-start | bytes 1228800 | tf_op jit(solution)/shard_map/reduce_scatter | solution.py:111
  437.2 18.9 %copy-start.6 = (bf16[2048,1024]{1,0:T(8,128)(2,1)S(1)}, bf16[2048,1024]{1,0:T(8,128)(2,1)}, u32[]{:S(2)}) copy-start(bf16[2048,1024]{1,0:T(8,128)(2,1)} %pad_maximum_fusion.2) | copy-start | bytes 12582916
  437.2 18.9 %slice-start.6 = ((s8[5242880]{0:T(1024)(128)(4,1)}), s8[4194304]{0:T(1024)(128)(4,1)S(1)}, s32[]{:S(2)}) async-start(s8[5242880]{0:T(1024)(128)(4,1)} %bitcast.158), calls=%async_computation.14 | async-start | bytes 8388608
  462.1 7.8 %copy-start.16 = (f32[2048,1280]{1,0:T(8,128)S(1)}, f32[2048,1280]{1,0:T(8,128)}, u32[]{:S(2)}) copy-start(f32[2048,1280]{1,0:T(8,128)} %convolution_add_fusion) | copy-start | bytes 31457284
  463.1 6.8 %copy-start.8 = (bf16[4,256,1280]{2,1,0:T(8,128)(2,1)S(1)}, bf16[4,256,1280]{2,1,0:T(8,128)(2,1)}, u32[]{:S(2)}) copy-start(bf16[4,256,1280]{2,1,0:T(8,128)(2,1)} %fusion.11) | copy-start | bytes 7864324
  463.5 13.9 %collective-permute-start.18 = (bf16[2,2,128,640]{3,2,1,0:T(8,128)(2,1)S(1)}, bf16[2,2,128,640]{3,2,1,0:T(8,128)(2,1)S(1)}, u32[]{:S(2)}, u32[]{:S(2)}) collective-permute-start(bf16[2,2,128,640]{3,2,1,0:T(8,128)(2,1)S(1)} %dynamic-slice_bitcast_fusion.1), channel_id=1, source_target_pairs={{0,4},{4,0},{8,12},{12,8},{16,20},{20,16},{24,28},{28,24},{1,5},{5... | collective-permute-start | bytes 1966088 | tf_op jit(solution)/shard_map/ppermute | solution.py:77
  469.8 8.2 %collective-permute-start.21 = (bf16[2,2,128,640]{3,2,1,0:T(8,128)(2,1)S(1)}, bf16[2,2,128,640]{3,2,1,0:T(8,128)(2,1)S(1)}, u32[]{:S(2)}, u32[]{:S(2)}) collective-permute-start(bf16[2,2,128,640]{3,2,1,0:T(8,128)(2,1)S(1)} %dynamic-slice_bitcast_fusion), channel_id=1, source_target_pairs={{0,4},{4,0},{8,12},{12,8},{16,20},{20,16},{24,28},{28,24},{1,5},{5... | collective-permute-start | bytes 1966088 | tf_op jit(solution)/shard_map/ppermute | solution.py:77
  477.7 12.6 %copy-start.1 = (f32[640,1280]{1,0:T(8,128)S(1)}, f32[640,1280]{1,0:T(8,128)}, u32[]{:S(2)}) copy-start(f32[640,1280]{1,0:T(8,128)} %param.12) | copy-start | bytes 9830404
  477.7 6.0 %collective-permute-start.19 = (bf16[2,128,640]{2,1,0:T(8,128)(2,1)S(1)}, bf16[2,128,640]{2,1,0:T(8,128)(2,1)S(1)}, u32[]{:S(2)}, u32[]{:S(2)}) collective-permute-start(bf16[2,128,640]{2,1,0:T(8,128)(2,1)S(1)} %dynamic-slice_bitcast_fusion.3), channel_id=1, source_target_pairs={{0,8},{4,12},{8,0},{12,4},{16,24},{20,28},{24,16},{28,20},{1,9},{5... | collective-permute-start | bytes 983048 | tf_op jit(solution)/shard_map/ppermute | solution.py:77
  478.2 6.9 %collective-permute-start.22 = (bf16[2,128,640]{2,1,0:T(8,128)(2,1)S(1)}, bf16[2,128,640]{2,1,0:T(8,128)(2,1)S(1)}, u32[]{:S(2)}, u32[]{:S(2)}) collective-permute-start(bf16[2,128,640]{2,1,0:T(8,128)(2,1)S(1)} %dynamic-slice_bitcast_fusion.2), channel_id=1, source_target_pairs={{0,16},{4,20},{8,24},{12,28},{16,0},{20,4},{24,8},{28,12},{1,17},{... | collective-permute-start | bytes 983048 | tf_op jit(solution)/shard_map/ppermute | solution.py:77
  483.8 6.3 %collective-permute-start.20 = (bf16[128,640]{1,0:T(8,128)(2,1)S(1)}, bf16[128,640]{1,0:T(8,128)(2,1)S(1)}, u32[]{:S(2)}, u32[]{:S(2)}) collective-permute-start(bf16[128,640]{1,0:T(8,128)(2,1)S(1)} %dynamic-slice_bitcast_fusion.5), channel_id=1, source_target_pairs={{0,16},{4,20},{8,24},{12,28},{16,0},{20,4},{24,8},{28,12},{1,17},{... | collective-permute-start | bytes 491528 | tf_op jit(solution)/shard_map/ppermute | solution.py:77
  485.2 5.0 collective-permute-start.23
  512.5 7.4 %copy-start.4 = (f32[256,1280]{1,0:T(8,128)S(1)}, f32[256,1280]{1,0:T(8,128)}, u32[]{:S(2)}) copy-start(f32[256,1280]{1,0:T(8,128)} %get-tuple-element.24) | copy-start | bytes 3932164
  512.6 7.4 %copy-start.5 = (f32[256,1280]{1,0:T(8,128)S(1)}, f32[256,1280]{1,0:T(8,128)}, u32[]{:S(2)}) copy-start(f32[256,1280]{1,0:T(8,128)} %get-tuple-element.32) | copy-start | bytes 3932164
  520.0 27.5 %copy-start.7 = (bf16[256,1280]{1,0:T(8,128)(2,1)S(1)}, bf16[256,1280]{1,0:T(8,128)(2,1)}, u32[]{:S(2)}) copy-start(bf16[256,1280]{1,0:T(8,128)(2,1)} %get-tuple-element.37) | copy-start | bytes 1966084
  542.5 17.3 %collective-permute-start.25 = (bf16[96,640]{1,0:T(8,128)(2,1)S(1)}, bf16[96,640]{1,0:T(8,128)(2,1)S(1)}, u32[]{:S(2)}, u32[]{:S(2)}) collective-permute-start(bf16[96,640]{1,0:T(8,128)(2,1)S(1)} %get-tuple-element.45), channel_id=1, source_target_pairs={{0,4},{1,12},{2,20},{3,28},{4,0},{5,8},{6,16},{7,24},{8,5},{9,13},... | collective-permute-start | bytes 368648 | tf_op jit(solution)/shard_map/ppermute | solution.py:123
  542.5 19.8 %collective-permute-start.24 = (bf16[96,640]{1,0:T(8,128)(2,1)S(1)}, bf16[96,640]{1,0:T(8,128)(2,1)S(1)}, u32[]{:S(2)}, u32[]{:S(2)}) collective-permute-start(bf16[96,640]{1,0:T(8,128)(2,1)S(1)} %get-tuple-element.46), channel_id=1, source_target_pairs={{0,0},{1,8},{2,16},{3,24},{4,4},{5,12},{6,20},{7,28},{8,1},{9,9},{... | collective-permute-start | bytes 368648 | tf_op jit(solution)/shard_map/ppermute | solution.py:123
  (7 other events, 26.2 us)
Sparse Core Ops, SparseCore 0:
  27.1 28.9 all-gather.3
  58.6 74.3 all-gather.5
  309.8 63.0 reduce-scatter.3
  437.0 67.9 reduce-scatter.5
  515.4 26.0 reduce-scatter.7
